TPU v7x, 32 devices: a whole 2x2x4 slice. The times are simulated.
32 devices in a mesh: ctx: 4 (over z), head: 8 (over y, x, core).
Axes of the slice: x: 2, y: 2, z: 4, core: 2. Of those that a mesh axis runs over, the one named last changes fastest.
Arguments:
- tokens_in: bfloat16 [1024, 4096], P('ctx', 'head'), may hold values from -6 to 6
- w_qkv: bfloat16 [4096, 8, 384], P(None, 'head'), may hold values from -0.125 to 0.125
- w_out: bfloat16 [8, 128, 4096], P('head'), may hold values from -0.75 to 0.75
- codebook: bfloat16 [8, 512, 128], P('head'), may hold values from -184 to 184
- codes: int32 [8, 1024], P('head', 'ctx'), may hold values from 0 to 511
- reach: int32 [4], P('ctx'), may hold values from 1 to 256, as said below
Outputs:
- mixed: bfloat16 [1024, 4096], P(('ctx', 'head'))
Inputs may be any that keep to these rules, and one draw needn't show every extreme that they name: reach[g] is how many of the last positions of block g - 1 block g sees with exact keys; reach[0] has no effect.
All inputs are finite; a program needn't handle non-finite values.
Results may differ from a plain program's by a relative error of at most 0.015.
Values may be sent and summed in bfloat16 or wider, within the bound.
A program may use at most 64 MiB of HBM per device.

v0:
```python
import math

import jax
import jax.numpy as jnp
from jax import lax
from jax.sharding import PartitionSpec as P

BLK = 256


def from_behind(block, axis, distance):
    devices = range(lax.axis_size(axis))
    route = [(i - distance, i) for i in devices if i - distance in devices]
    return lax.ppermute(block, axis, route)


def entering(value, axis, combine, identity):
    devices, index = (lax.axis_size(axis), lax.axis_index(axis))
    everything = jax.tree.map(
        lambda part, kind: lax.all_gather(part.astype(kind), axis),
        value,
        (jnp.bfloat16, jnp.bfloat16),
    )
    start = jax.tree.map(
        lambda part, zero: jnp.broadcast_to(jnp.asarray(zero, part.dtype), part.shape),
        value,
        identity,
    )

    def turn(k, before):
        reached = k < index
        new = combine(
            before, jax.tree.map(lambda part, own: part[k].astype(own.dtype), everything, value)
        )
        return jax.tree.map(lambda a, b: jnp.where(reached, a, b), new, before)

    return lax.fori_loop(0, devices, turn, start)


def attend_block(
    queries, keys_win, vals_win, cache_v, cache_c, book, reach_one, prev_flag, block_len, scale
):
    exact = (
        lax.dot_general(
            queries, keys_win, (((1,), (1,)), ((), ())), preferred_element_type=jnp.float32
        )
        * scale
    )
    coded = (
        lax.dot_general(queries, book, (((1,), (1,)), ((), ())), preferred_element_type=jnp.float32)
        * scale
    )
    rows = lax.broadcasted_iota(jnp.int32, exact.shape, 0)
    cols = lax.broadcasted_iota(jnp.int32, exact.shape, 1)
    prev_ok = (cols < block_len) & (cols >= block_len - reach_one) & prev_flag
    curr_ok = (cols >= block_len) & (cols - block_len <= rows)
    allowed = prev_ok | curr_ok
    valid = cache_c > 0.5
    top = jnp.maximum(
        jnp.max(jnp.where(allowed, exact, -jnp.inf), axis=1),
        jnp.max(jnp.where(valid[None, :], coded, -jnp.inf), axis=1),
    )
    probs = jnp.exp(jnp.where(allowed, exact - top[:, None], -jnp.inf))
    weights = jnp.exp(jnp.where(valid[None, :], coded - top[:, None], -jnp.inf))
    numer = jnp.dot(probs.astype(jnp.bfloat16), vals_win, preferred_element_type=jnp.float32)
    numer = numer + jnp.dot(weights, cache_v, precision=lax.Precision.HIGHEST)
    denom = jnp.sum(probs, axis=1) + jnp.dot(weights, cache_c, precision=lax.Precision.HIGHEST)
    return (numer / denom[:, None]).astype(jnp.bfloat16)


def combine(earlier, later):
    return (earlier[0] + later[0], earlier[1] + later[1])


def on_device(tokens_in, w_qkv, w_out, codebook, codes, reach):
    tok_rows = tokens_in.shape[0]
    head_dim = codebook.shape[2]
    num_codes = codebook.shape[1]
    num_blocks = tok_rows // BLK
    scale = 1.0 / math.sqrt(head_dim)
    w_local = w_qkv[:, 0, :]
    projected = jnp.dot(
        lax.all_gather(tokens_in, "head", axis=1, tiled=True),
        w_local,
        preferred_element_type=jnp.float32,
    )
    queries = projected[:, :head_dim].astype(jnp.bfloat16)
    key_vals = projected[:, head_dim:].astype(jnp.bfloat16)
    code_row = codes[0]
    book = codebook[0]
    prev_kv, prev_codes = from_behind((key_vals, code_row), "ctx", 1)
    has_prev = lax.axis_index("ctx") > 0
    code_ids = jnp.arange(num_codes, dtype=jnp.int32)
    onehot_loc = (code_row[:, None] == code_ids[None, :]).astype(jnp.bfloat16)
    local_v = jnp.einsum(
        "ts,td->sd", onehot_loc, key_vals[:, head_dim:], preferred_element_type=jnp.float32
    )
    local_c = jnp.sum(onehot_loc, axis=0, dtype=jnp.float32)
    before_v, before_c = entering(
        (local_v, local_c), "ctx", combine, (jnp.zeros_like(local_v), jnp.zeros_like(local_c))
    )
    ext_kv = jnp.concatenate([prev_kv, key_vals], axis=0)
    ext_codes = jnp.concatenate([prev_codes, code_row], axis=0)
    ext_len = BLK + tok_rows
    positions = jnp.arange(ext_len, dtype=jnp.int32)[:, None]
    thresholds = (jnp.arange(num_blocks, dtype=jnp.int32) + 1) * BLK - reach
    plus = (positions >= BLK) & (positions < thresholds[None, :])
    minus = (positions < BLK) & (positions >= thresholds[None, :]) & has_prev
    signs = (plus.astype(jnp.float32) - minus.astype(jnp.float32)).astype(jnp.bfloat16)
    signed_vals = (signs[:, :, None] * ext_kv[:, None, head_dim:]).reshape(
        ext_len, num_blocks * head_dim
    )
    onehot_ext = (ext_codes[:, None] == code_ids[None, :]).astype(jnp.bfloat16)
    part_v = jnp.einsum(
        "es,ef->sf", onehot_ext, signed_vals, preferred_element_type=jnp.float32
    ).reshape(num_codes, num_blocks, head_dim)
    part_c = jnp.einsum("es,eb->sb", onehot_ext, signs, preferred_element_type=jnp.float32)
    cache_v = before_v + part_v[:, 0, :]
    cache_c = before_c + part_c[:, 0]
    prev_flag = has_prev | (0 > 0)
    pieces_out = attend_block(
        queries,
        ext_kv[:, :head_dim],
        ext_kv[:, head_dim:],
        cache_v,
        cache_c,
        book,
        reach[0],
        prev_flag,
        BLK,
        scale,
    )
    w_proj = w_out[0]
    mixed = lax.psum_scatter(
        jnp.dot(pieces_out, w_proj, preferred_element_type=jnp.float32).astype(jnp.bfloat16),
        "head",
        scatter_dimension=0,
        tiled=True,
    )
    return mixed


def solution(mesh):
    in_specs = (
        P("ctx", "head"),
        P(None, "head", None),
        P("head", None, None),
        P("head", None, None),
        P("head", "ctx"),
        P("ctx"),
    )
    out_specs = P(("ctx", "head"), None)
    return jax.shard_map(
        on_device, mesh=mesh, in_specs=in_specs, out_specs=out_specs, check_vma=False
    )
```

profile of v0, /device:TPU:25, one launch (start us, length us, event | category | flops | bytes accessed | tf_op | source)
XLA Modules:
  0.0 124.3 jit_solution(7663660152165081408)
XLA Ops:
  6.5 0.0 copy-start
  6.5 0.0 all-gather.5.cloned.1.call-start
  6.5 0.7 all-gather.5.cloned.1.call-update
  7.3 0.0 reduce-scatter.2.cloned.1.call-start
  7.3 1.4 %collective-permute-start.1 = (s32[256]{0:T(256)}, s32[256]{0:T(256)S(1)}, u32[]{:S(2)}, u32[]{:S(2)}) collective-permute-start(s32[256]{0:T(256)} %bitcast.39), channel_id=1, source_target_pairs={{0,8},{8,16},{16,24},{1,9},{9,17},{17,25},{2,10},{10,18},{18,26},{... | collective-permute-start | bytes 3080 | tf_op jit(solution)/shard_map/ppermute | solution.py:14
  9.4 0.8 fusion.20
  10.2 0.0 copy-start.4
  10.3 0.6 iota_compare_fusion.6
  10.9 0.0 copy-done.4
  10.9 8.3 %all-gather.2 = bf16[4,1,512]{2,1,0:T(2,128)(2,1)S(1)} all-gather(bf16[1,1,512]{2,1,0:T(2,128)(2,1)S(1)} %reshape.63), channel_id=3, replica_groups=mesh['ctx'=4,'head'=8] {'ctx'}, dimensions={0}, use_global_device_ids=true | all-gather | bytes 5120 | tf_op jit(solution)/shard_map/all_gather | solution.py:20
  19.2 0.0 collective-permute-done.1
  19.2 0.7 pad_add_fusion
  19.9 0.0 copy-start.6
  19.9 0.9 fusion.8
  20.8 18.1 %all-gather.5.cloned.1.call-done = bf16[256,4096]{1,0:T(8,128)(2,1)} async-done(((bf16[256,512]{1,0:T(8,128)(2,1)}), bf16[256,4096]{1,0:T(8,128)(2,1)}) %all-gather.5.cloned.1.call-update) | async-done | bytes 2097168 | tf_op jit(solution)/shard_map/all_gather | solution.py:83
  38.9 0.0 copy-done.6
  38.9 0.0 copy-done
  38.9 0.0 copy-start.5
  38.9 2.9 %fusion.2 = bf16[256,384]{1,0:T(8,128)(2,1)S(1)} fusion(bf16[256,4096]{1,0:T(8,128)(2,1)} %all-gather.5.cloned.1.call-done, bf16[4096,1,384]{2,0,1:T(8,128)(2,1)S(1)} %copy-done), kind=kOutput, calls=%fused_computation.8 | convolution fusion | flops 805404672 | bytes 5439488 | tf_op jit(solution)/shard_map/dot_general | solution.py:82
  41.7 0.0 copy-start.2
  41.8 0.6 copy-done.2
  42.4 0.0 copy-done.5
  42.4 0.4 convolution_convert_fusion.1
  42.8 1.3 %collective-permute-start = (bf16[256,256]{1,0:T(8,128)(2,1)S(1)}, bf16[256,256]{1,0:T(8,128)(2,1)}, u32[]{:S(2)}, u32[]{:S(2)}) collective-permute-start(bf16[256,256]{1,0:T(8,128)(2,1)S(1)} %slice.25), channel_id=1, source_target_pairs={{0,8},{8,16},{16,24},{1,9},{9,17},{17,25},{2,10},{10,18},{18,26},{... | collective-permute-start | bytes 393224 | tf_op jit(solution)/shard_map/ppermute | solution.py:14
  44.1 15.0 %all-gather = bf16[2048,128]{1,0:T(8,128)(2,1)} all-gather(bf16[512,128]{1,0:T(8,128)(2,1)S(1)} %convolution_convert_fusion.1), channel_id=2, replica_groups=mesh['ctx'=4,'head'=8] {'ctx'}, dimensions={0}, use_global_device_ids=true | all-gather | bytes 655360 | tf_op jit(solution)/shard_map/all_gather | solution.py:20
  59.1 4.4 %while.16 = (s32[]{:T(128)}, f32[512,128]{1,0:T(8,128)S(1)}, f32[512]{0:T(512)S(1)}, s32[]{:T(128)}, bf16[4,512,128]{2,1,0:T(8,128)(2,1)}, /*index=5*/bf16[4,512]{1,0:T(4,128)(2,1)S(1)}, s32[]{:T(128)}, s32[]{:T(128)}) while((s32[]{:T(128)}, f32[512,128]{1,0:T(8,128)S(1)}, f32[512]{0:T(512)S(1)}, s32[]{:T(128)}, ...), condition=%wide.region_3.4_spmd.clone, body=%wide.region_2.3_spmd.clone.sunk | while | flops 264196 | bytes 664699 | solution.py:37
  59.1 1.0 add_select_fusion.4
  60.2 1.0 add_select_fusion.4
  61.3 1.0 add_select_fusion.4
  62.4 1.0 add_select_fusion.4
  63.5 0.7 broadcast_compare_fusion
  64.2 0.0 copy-start.3
  64.2 1.2 %select_reduce_fusion = (f32[256]{0:T(256)S(1)}, f32[256,512]{1,0:T(8,128)S(1)}) fusion(pred[512]{0:T(512)(128)(4,1)S(1)} %get-tuple-element.150, bf16[1,512,128]{2,1,0:T(8,128)(2,1)} %param.11, bf16[256,384]{1,0:T(8,128)(2,1)} %copy-done.2), kind=kOutput, calls=%fused_computation.19 | convolution fusion | flops 33947392 | bytes 722432 | tf_op jit(solution)/shard_map/dot_general | solution.py:50
  65.4 0.0 collective-permute-done
  65.4 1.2 select_reduce_fusion.1
  66.6 0.0 copy-start.1
  66.6 1.6 %convolution_add_fusion = f32[512,128]{1,0:T(8,128)S(1)} fusion(f32[512,128]{1,0:T(8,128)S(1)} %get-tuple-element.116, s32[512]{0:T(512)} %copy-done.6, bf16[512]{0:T(512)(128)(2,1)} %copy-done.4, bf16[256,256]{1,0:T(8,128)(2,1)S(1)} %slice.25, bf16[256,256]{1,0:T(8,128)(2,1)} %collective-permute-done), kind=kOutput, calls=%fused_computation.9 | convolution fusion | flops 67829760 | bytes 789504 | tf_op jit(solution)/shard_map/es,ef->sf/dot_general | solution.py:114
  68.2 0.6 fusion.15
  68.9 0.6 fusion.14
  69.5 0.0 copy-done.1
  69.5 0.0 copy-done.3
  69.5 0.3 fusion.16
  69.8 3.7 %convolution_convert_fusion = bf16[256,4096]{1,0:T(8,128)(2,1)} fusion(f32[256,128]{1,0:T(8,128)S(1)} %fusion.15, bf16[1,128,4096]{2,1,0:T(8,128)(2,1)} %param.10, f32[256,512]{1,0:T(8,128)} %copy-done.1, f32[256]{0:T(256)S(1)} %max.7, s32[512]{0:T(512)S(1)} %iota_add_fusion, pred[512]{0:T(512)(128)(4,1)S(1)} %get-tuple-element.156, ...), kind=kOutput, calls=%fused_computation.3 | convolution fusion | flops 304185344 | bytes 4068352 | tf_op jit(solution)/shard_map/dot_general | solution.py:135
  73.5 0.0 reduce-scatter.2.cloned.1.call-update
  73.6 43.9 %reduce-scatter.2.cloned.1.call-done = bf16[32,4096]{1,0:T(8,128)(2,1)} async-done(((bf16[256,4096]{1,0:T(8,128)(2,1)}), bf16[32,4096]{1,0:T(8,128)(2,1)}) %reduce-scatter.2.cloned.1.call-update) | async-done | bytes 262160 | tf_op jit(solution)/shard_map/reduce_scatter | solution.py:134
  (18 shorter events, 0.1 us)
Async XLA Ops:
  6.5 32.3 %copy-start = (bf16[4096,1,384]{2,0,1:T(8,128)(2,1)S(1)}, bf16[4096,1,384]{2,0,1:T(8,128)(2,1)}, u32[]{:S(2)}) copy-start(bf16[4096,1,384]{2,0,1:T(8,128)(2,1)} %param.9) | copy-start | bytes 9437188
  6.5 32.3 %all-gather.5.cloned.1.call-start = ((), (), s32[]{:S(2)}) async-start(), calls=%async_computation.1 | async-start | bytes 2359296 | tf_op jit(solution)/shard_map/all_gather | solution.py:83
  7.3 110.2 %reduce-scatter.2.cloned.1.call-start = ((), (), s32[]{:S(2)}) async-start(), calls=%async_computation.2 | async-start | bytes 2359296 | tf_op jit(solution)/shard_map/reduce_scatter | solution.py:134
  7.3 11.9 %collective-permute-start.1 = (s32[256]{0:T(256)}, s32[256]{0:T(256)S(1)}, u32[]{:S(2)}, u32[]{:S(2)}) collective-permute-start(s32[256]{0:T(256)} %bitcast.39), channel_id=1, source_target_pairs={{0,8},{8,16},{16,24},{1,9},{9,17},{17,25},{2,10},{10,18},{18,26},{... | collective-permute-start | bytes 3080 | tf_op jit(solution)/shard_map/ppermute | solution.py:14
  10.2 0.6 copy-start.4
  19.9 19.0 %copy-start.6 = (s32[512]{0:T(512)}, s32[512]{0:T(512)S(1)}, u32[]{:S(2)}) copy-start(s32[512]{0:T(512)S(1)} %pad_add_fusion) | copy-start | bytes 6148
  38.9 3.5 %copy-start.5 = (s32[1,256]{1,0:T(1,128)S(1)}, s32[1,256]{1,0:T(1,128)}, u32[]{:S(2)}) copy-start(s32[1,256]{1,0:T(1,128)} %param.12) | copy-start | bytes 3076
  41.7 0.7 copy-start.2
  42.8 22.6 %collective-permute-start = (bf16[256,256]{1,0:T(8,128)(2,1)S(1)}, bf16[256,256]{1,0:T(8,128)(2,1)}, u32[]{:S(2)}, u32[]{:S(2)}) collective-permute-start(bf16[256,256]{1,0:T(8,128)(2,1)S(1)} %slice.25), channel_id=1, source_target_pairs={{0,8},{8,16},{16,24},{1,9},{9,17},{17,25},{2,10},{10,18},{18,26},{... | collective-permute-start | bytes 393224 | tf_op jit(solution)/shard_map/ppermute | solution.py:14
  64.2 5.4 %copy-start.3 = (pred[512]{0:T(512)(128)(4,1)S(1)}, pred[512]{0:T(512)(128)(4,1)}, u32[]{:S(2)}) copy-start(pred[512]{0:T(512)(128)(4,1)} %get-tuple-element.157) | copy-start | bytes 1540
  66.6 2.9 %copy-start.1 = (f32[256,512]{1,0:T(8,128)}, f32[256,512]{1,0:T(8,128)S(1)}, u32[]{:S(2)}) copy-start(f32[256,512]{1,0:T(8,128)S(1)} %get-tuple-element.153) | copy-start | bytes 1572868
Sparse Core Ops, SparseCore 0:
  9.2 29.5 all-gather.4
  73.7 43.7 reduce-scatter.1
where the time goes:
time: 127 us; the launch traced here: 124 us
  waiting for transfers between devices  62.7 us (49%)
  blocking collectives  23.3 us (18%)
  between operations  14.2 us (11%)
  matrix products  13.2 us (10%)
  other arithmetic  7.32 us (6%)
  starting transfers between devices  2.76 us (2%)
    reduce_scatter x1, waiting for transfers between devices, on_device(): lax.psum_scatter(jnp.dot(pieces_out, w_proj, preferred_element_type=jnp.f...  43.9 us
    all_gather x2, blocking collectives, entering(): lax.all_gather(part.astype(kind), axis)  23.3 us
    all_gather x1, waiting for transfers between devices, on_device(): lax.all_gather(tokens_in, 'head', axis=1, tiled=True)  18.1 us
    select_n x8, other arithmetic, turn(): return jax.tree.map(lambda a, b: jnp.where(reached, a, b), new, before)  4.22 us
    dot_general x1, matrix products, on_device(): jnp.dot(pieces_out, w_proj, preferred_element_type=jnp.float32)  3.71 us
    dot_general x1, matrix products, on_device(): jnp.dot(lax.all_gather(tokens_in, 'head', axis=1, tiled=True), w_local, p...  2.85 us
    ppermute x2, starting transfers between devices, from_behind(): return lax.ppermute(block, axis, route)  2.72 us
  transfers between devices with their start and end apart: 4, of which 2 were waited for; matrix products, arithmetic and copies ran while one was open for 7% of the time, Pallas kernels for 0%

commit v1 on v0

v1 whole, which is shorter than its diff:
```python
import functools
import math

import jax
import jax.numpy as jnp
from jax import lax
from jax.experimental import pallas as pl
from jax.experimental.pallas import tpu as pltpu
from jax.sharding import PartitionSpec as P

MESH = pl.DeviceIdType.MESH
F32 = jnp.float32
BF16 = jnp.bfloat16
ROW_CHUNKS = 2
COL_CHUNKS = 4


def grid_of(chips):
    wide = 1 << ((chips.bit_length() - 1) // 2)
    return chips // wide, wide


def nt(a, b):
    return lax.dot_general(a, b, (((1,), (1,)), ((), ())), preferred_element_type=F32)


def kernel(
    sizes,
    tok, w_in, w_out, book, codes, reach, out,
    x, w, w2, book_v, codes_v, reach_s, kq, kz, vz, q_s, top_s, den_s, acc_s, att, att_p, term, got,
    local_sem, ag_send, ag_recv, fw_send, fw_recv, w2_sem, kq_send, kq_recv, k_send, k_recv,
    v_send, v_recv, att_sem, rs_send, rs_recv,
):
    ctxs, heads, blk, hd = sizes
    chips = heads // 2
    tall, wide = grid_of(chips)
    scale = 1.0 / math.sqrt(hd)
    rows = blk // ROW_CHUNKS
    cols = out.shape[1] // COL_CHUNKS
    rp = out.shape[0]
    ctx, head = lax.axis_index("ctx"), lax.axis_index("head")
    chip, core = head // 2, head % 2
    partner = (ctx, chip * 2 + 1 - core)

    def chip_at(d, sign):
        up, across = d // wide, d % wide
        row = lax.rem(chip // wide + (up if sign > 0 else tall - up), tall)
        col = lax.rem(chip % wide + (across if sign > 0 else wide - across), wide)
        return row * wide + col

    def remote(src, dst, send, recv, to):
        return pltpu.make_async_remote_copy(
            src_ref=src, dst_ref=dst, send_sem=send, recv_sem=recv, device_id=to, device_id_type=MESH
        )

    def arrived(dst, sem):
        remote(dst, dst, sem, sem, partner).wait_recv()

    copies = [
        pltpu.make_async_copy(codes, codes_v, local_sem.at[0]),
        pltpu.make_async_copy(book, book_v, local_sem.at[1]),
        pltpu.make_async_copy(reach, reach_s, local_sem.at[2]),
        pltpu.make_async_copy(tok, x.at[0, 0], local_sem.at[3]),
        pltpu.make_async_copy(w_in, w, local_sem.at[4]),
        pltpu.make_async_copy(w_out, w2.at[pl.ds(0, hd)], local_sem.at[5]),
    ]
    for copy in copies:
        copy.start()

    barrier = pltpu.get_barrier_semaphore()
    greet = [partner]
    greet += [(ctx, chip_at(d, 1) * 2 + core) for d in range(1, chips)]
    greet += [(lax.rem(ctx + e, ctxs), head) for e in range(1, ctxs)]
    for peer in greet:
        pl.semaphore_signal(barrier, inc=1, device_id=peer, device_id_type=MESH)
    pl.semaphore_wait(barrier, len(greet))

    sends = []

    def send(*args):
        copy = remote(*args)
        copy.start()
        sends.append(copy)

    def part(r):
        return pl.ds(r * rows, rows)

    for r in range(ROW_CHUNKS):
        for d in range(1, chips):
            to = (ctx, chip_at(d, 1) * 2 + core)
            send(tok.at[part(r)], x.at[d, 0, part(r)], ag_send.at[r, d], ag_recv.at[r, d], to)
        send(tok.at[part(r)], x.at[0, 1, part(r)], fw_send.at[r, 0], fw_recv.at[r, 0], partner)
    send(w_out, w2.at[pl.ds(hd, hd)], w2_sem.at[0], w2_sem.at[1], partner)

    copies[0].wait()
    copies[1].wait()
    num_codes = book_v.shape[0]
    hot = lax.broadcasted_iota(jnp.int32, (num_codes, blk), 0) == codes_v[...]
    kq[0] = lax.dot_general(
        hot.astype(F32).astype(BF16), book_v[...], (((0,), (0,)), ((), ())), preferred_element_type=F32
    ).astype(BF16)

    def later(e, src, dst, send_sem, recv_sem):
        @pl.when(ctx + e < ctxs)
        def _():
            remote(src, dst, send_sem, recv_sem, (lax.rem(ctx + e, ctxs), head)).start()

    for e in range(1, ctxs):
        later(e, kq.at[0], kq.at[e], kq_send.at[e], kq_recv.at[e])

    for copy in copies[2:]:
        copy.wait()

    for r in range(ROW_CHUNKS):
        def piece(d, other):
            source = chip_at(d, -1) * 2 + (1 - core if other else core)
            return jnp.dot(x[d, other, r * rows:(r + 1) * rows], w[source], preferred_element_type=F32)

        proj = piece(0, 0)
        arrived(x.at[0, 1, part(r)], fw_recv.at[r, 0])
        proj += piece(0, 1)
        for d in range(1, chips):
            arrived(x.at[d, 0, part(r)], ag_recv.at[r, d])
            send(x.at[d, 0, part(r)], x.at[d, 1, part(r)], fw_send.at[r, d], fw_recv.at[r, d], partner)
            proj += piece(d, 0)
        for d in range(1, chips):
            arrived(x.at[d, 1, part(r)], fw_recv.at[r, d])
            proj += piece(d, 1)
        q_s[r * rows:(r + 1) * rows] = proj[:, :hd].astype(BF16)
        kz[0, r * rows:(r + 1) * rows] = proj[:, hd:2 * hd].astype(BF16)
        vz[0, r * rows:(r + 1) * rows] = proj[:, 2 * hd:].astype(BF16)
        later(1, kz.at[0, part(r)], kz.at[1, part(r)], k_send.at[r], k_recv.at[r])
        for e in range(1, ctxs):
            later(e, vz.at[0, part(r)], vz.at[e, part(r)], v_send.at[r, e], v_recv.at[r, e])

    queries = q_s[...]
    scores = nt(queries, kz[0])
    seen = lax.broadcasted_iota(jnp.int32, scores.shape, 1) <= lax.broadcasted_iota(
        jnp.int32, scores.shape, 0
    )
    scores = jnp.where(seen, scores, -jnp.inf)
    top = jnp.max(scores, axis=1, keepdims=True)
    probs = jnp.exp((scores - top) * scale)
    top_s[...] = jnp.broadcast_to(top, top_s.shape)
    den_s[...] = jnp.broadcast_to(jnp.sum(probs, axis=1, keepdims=True), den_s.shape)
    acc_s[...] = jnp.dot(probs.astype(BF16), vz[0], preferred_element_type=F32)

    for e in range(1, ctxs):
        @pl.when(ctx >= e)
        def _():
            arrived(kq.at[e], kq_recv.at[e])
            keys = kq[e]
            if e == 1:
                for r in range(ROW_CHUNKS):
                    arrived(kz.at[1, part(r)], k_recv.at[r])
                position = lax.broadcasted_iota(jnp.int32, keys.shape, 0)
                keys = jnp.where(position >= blk - reach_s[0], kz[1], keys)
            scores = nt(q_s[...], keys)
            old = top_s[...][:, :1]
            top = jnp.maximum(old, jnp.max(scores, axis=1, keepdims=True))
            fade = jnp.exp((old - top) * scale)
            probs = jnp.exp((scores - top) * scale)
            for r in range(ROW_CHUNKS):
                arrived(vz.at[e, part(r)], v_recv.at[r, e])
            top_s[...] = jnp.broadcast_to(top, top_s.shape)
            den_s[...] = den_s[...] * fade + jnp.sum(probs, axis=1, keepdims=True)
            acc_s[...] = acc_s[...] * fade + jnp.dot(
                probs.astype(BF16), vz[e], preferred_element_type=F32
            )

    attended = acc_s[...] / den_s[...]
    for h in range(heads):
        att[h % 2, h // 2] = attended[h * rp:(h + 1) * rp].astype(BF16)
    send(att.at[1 - core], att_p, att_sem.at[0], att_sem.at[1], partner)
    mine = att[core].astype(F32).reshape(chips * rp, hd).astype(BF16)
    arrived(att_p, att_sem.at[1])
    other = att_p[...].astype(F32).reshape(chips * rp, hd).astype(BF16)
    arrived(w2.at[pl.ds(hd, hd)], w2_sem.at[1])
    both = jnp.concatenate([mine, other], axis=1)

    for j in range(COL_CHUNKS):
        block = jnp.dot(both, w2[:, j * cols:(j + 1) * cols], preferred_element_type=F32)
        for c in range(chips):
            term[j, c] = block[c * rp:(c + 1) * rp].astype(BF16)
        for d in range(1, chips):
            peer = chip_at(d, 1)
            send(term.at[j, peer], got.at[j, d], rs_send.at[j, d], rs_recv.at[j, d], (ctx, peer * 2 + core))

    for j in range(COL_CHUNKS):
        total = term[j, chip].astype(F32)
        for d in range(1, chips):
            arrived(got.at[j, d], rs_recv.at[j, d])
            total += got[j, d].astype(F32)
        out[:, j * cols:(j + 1) * cols] = total.astype(BF16)

    for copy in sends:
        copy.wait_send()
    for e in range(1, ctxs):
        @pl.when(ctx + e < ctxs)
        def _():
            remote(kq.at[0], kq.at[e], kq_send.at[e], kq_recv.at[e], partner).wait_send()
            for r in range(ROW_CHUNKS):
                if e == 1:
                    remote(kz.at[0, part(r)], kz.at[1, part(r)], k_send.at[r], k_recv.at[r], partner).wait_send()
                remote(
                    vz.at[0, part(r)], vz.at[e, part(r)], v_send.at[r, e], v_recv.at[r, e], partner
                ).wait_send()


def solution(mesh):
    ctxs, heads = mesh.shape["ctx"], mesh.shape["head"]
    chips = heads // 2

    def on_device(tokens_in, w_qkv, w_out, codebook, codes, reach):
        blk, depth = tokens_in.shape
        num_codes, hd = codebook.shape[1:]
        wide = w_out.shape[2]
        rp = blk // heads
        cols = wide // COL_CHUNKS
        dma = pltpu.SemaphoreType.DMA
        return pl.pallas_call(
            functools.partial(kernel, (ctxs, heads, blk, hd)),
            out_shape=jax.ShapeDtypeStruct((rp, wide), BF16),
            in_specs=[pl.BlockSpec(memory_space=pl.ANY)] * 6,
            out_specs=pl.BlockSpec(memory_space=pltpu.VMEM),
            scratch_shapes=[
                pltpu.VMEM((chips, 2, blk, depth), BF16),
                pltpu.VMEM((heads, depth, 3 * hd), BF16),
                pltpu.VMEM((2 * hd, wide), BF16),
                pltpu.VMEM((num_codes, hd), BF16),
                pltpu.VMEM((1, blk), jnp.int32),
                pltpu.SMEM((1,), jnp.int32),
                pltpu.VMEM((ctxs, blk, hd), BF16),
                pltpu.VMEM((2, blk, hd), BF16),
                pltpu.VMEM((ctxs, blk, hd), BF16),
                pltpu.VMEM((blk, hd), BF16),
                pltpu.VMEM((blk, hd), F32),
                pltpu.VMEM((blk, hd), F32),
                pltpu.VMEM((blk, hd), F32),
                pltpu.VMEM((2, chips, rp, hd), BF16),
                pltpu.VMEM((chips, rp, hd), BF16),
                pltpu.VMEM((COL_CHUNKS, chips, rp, cols), BF16),
                pltpu.VMEM((COL_CHUNKS, chips, rp, cols), BF16),
                dma((6,)),
                dma((ROW_CHUNKS, chips)),
                dma((ROW_CHUNKS, chips)),
                dma((ROW_CHUNKS, chips)),
                dma((ROW_CHUNKS, chips)),
                dma((2,)),
                dma((ctxs,)),
                dma((ctxs,)),
                dma((ROW_CHUNKS,)),
                dma((ROW_CHUNKS,)),
                dma((ROW_CHUNKS, ctxs)),
                dma((ROW_CHUNKS, ctxs)),
                dma((2,)),
                dma((COL_CHUNKS, chips)),
                dma((COL_CHUNKS, chips)),
            ],
            compiler_params=pltpu.CompilerParams(
                collective_id=0, has_side_effects=True, vmem_limit_bytes=48 * 1024 * 1024
            ),
            cost_estimate=pl.CostEstimate(
                flops=2 * blk * heads * depth * 3 * hd, bytes_accessed=6 * 1024 * 1024, transcendentals=blk * blk
            ),
        )(
            tokens_in, w_qkv[:, 0, :].reshape(heads, depth, 3 * hd), w_out[0], codebook[0], codes, reach
        )

    in_specs = (
        P("ctx", "head"),
        P(None, "head", None),
        P("head", None, None),
        P("head", None, None),
        P("head", "ctx"),
        P("ctx"),
    )
    return jax.shard_map(
        on_device, mesh=mesh, in_specs=in_specs, out_specs=P(("ctx", "head"), None), check_vma=False
    )
```

time: 127 us -> 46.1 us (0.36); the launches traced: 124 us -> 45.8 us
  waiting for transfers between devices: 62.7 us -> 0 us
  Pallas kernels: 0 us -> 38.8 us
  blocking collectives: 23.3 us -> 0 us
  between operations: 14.2 us -> 0.67 us
  matrix products: 13.2 us -> 0 us
  other arithmetic: 7.32 us -> 0 us
  local copies, waits for them, and re-layouts: 0.72 us -> 6.34 us
  starting transfers between devices: 2.76 us -> 0 us
    reduce_scatter x1 -> x0, waiting for transfers between devices: 43.9 us -> none  [on_device(): lax.psum_scatter(jnp.dot(pieces_out, w_proj, preferred_element_type=jnp.f...]
    pallas_call x0 -> x1, Pallas kernels: none -> 38.8 us  [on_device(): pl.pallas_call(functools.partial(kernel, (ctxs, heads, blk, hd)), out_sha...]
    all_gather x2 -> x0, blocking collectives: 23.3 us -> none  [entering(): lax.all_gather(part.astype(kind), axis)]
    all_gather x1 -> x0, waiting for transfers between devices: 18.1 us -> none  [on_device(): lax.all_gather(tokens_in, 'head', axis=1, tiled=True)]
    dot_general x9 -> x0, matrix products: 13.2 us -> none  [the longest x1 3.71 us: on_device(): jnp.dot(pieces_out, w_proj, preferred_element_type=jnp.float32)]
    unnamed x16 -> x11, local copies, waits for them, and re-layouts: 0.7 us -> 6.34 us
    select_n x8 -> x0, other arithmetic: 4.22 us -> none  [turn(): return jax.tree.map(lambda a, b: jnp.where(reached, a, b), new, before)]
    ppermute x2 -> x0, starting transfers between devices: 2.72 us -> none  [from_behind(): return lax.ppermute(block, axis, route)]
  transfers between devices with their start and end apart: 4 -> 0, of which waited for: 2 -> 0; matrix products, arithmetic and copies ran while one was open for 7% -> 0% of each run, Pallas kernels for 0% -> 0%
where the time goes in v1:
time: 46.1 us; the launch traced here: 45.8 us
  Pallas kernels  38.8 us (84%)
  local copies, waits for them, and re-layouts  6.34 us (14%)
  between operations  0.67 us (1%)
    pallas_call x1, Pallas kernels, on_device(): pl.pallas_call(functools.partial(kernel, (ctxs, heads, blk, hd)), out_sha...  38.8 us
    unnamed x11, local copies, waits for them, and re-layouts  6.34 us

profile of v1, /device:TPU:25, one launch (start us, length us, event | category | flops | bytes accessed | tf_op | source)
XLA Modules:
  0.0 45.8 jit_solution(9657237328817405253)
XLA Ops:
  0.7 0.0 copy-start
  0.7 1.9 %copy-done = bf16[4096,1,384]{2,0,1:T(8,128)(2,1)S(1)} copy-done((bf16[4096,1,384]{2,0,1:T(8,128)(2,1)S(1)}, bf16[4096,1,384]{2,0,1:T(8,128)(2,1)}, u32[]{:S(2)}) %copy-start) | copy-done | bytes 3145752
  2.5 0.0 copy-start.1
  2.5 1.2 %copy-done.1 = bf16[1,128,4096]{2,1,0:T(8,128)(2,1)S(1)} copy-done((bf16[1,128,4096]{2,1,0:T(8,128)(2,1)S(1)}, bf16[1,128,4096]{2,1,0:T(8,128)(2,1)}, u32[]{:S(2)}) %copy-start.1) | copy-done | bytes 1048600
  3.8 0.0 copy-start.2
  3.8 0.9 %copy-done.2 = bf16[256,512]{1,0:T(8,128)(2,1)S(1)} copy-done((bf16[256,512]{1,0:T(8,128)(2,1)S(1)}, bf16[256,512]{1,0:T(8,128)(2,1)}, u32[]{:S(2)}) %copy-start.2) | copy-done | bytes 262168
  4.7 0.0 copy-start.3
  4.7 0.9 %copy-done.3 = bf16[1,512,128]{2,1,0:T(8,128)(2,1)S(1)} copy-done((bf16[1,512,128]{2,1,0:T(8,128)(2,1)S(1)}, bf16[1,512,128]{2,1,0:T(8,128)(2,1)}, u32[]{:S(2)}) %copy-start.3) | copy-done | bytes 131096
  5.6 0.0 copy-start.4
  5.6 0.7 %copy-done.4 = s32[1,256]{1,0:T(1,128)S(1)} copy-done((s32[1,256]{1,0:T(1,128)S(1)}, s32[1,256]{1,0:T(1,128)}, u32[]{:S(2)}) %copy-start.4) | copy-done | bytes 1048
  6.3 38.8 %shard_map.64 = bf16[32,4096]{1,0:T(8,128)(2,1)S(1)} custom-call(bf16[256,512]{1,0:T(8,128)(2,1)S(1)} %copy-done.2, bf16[8,512,384]{2,1,0:T(8,128)(2,1)S(1)} %bitcast.3, bf16[128,4096]{1,0:T(8,128)(2,1)S(1)} %bitcast.4, bf16[512,128]{1,0:T(8,128)(2,1)S(1)} %bitcast.5, s32[1,256]{1,0:T(1,128)S(1)} %copy-done.4, s32[1]{0:T(128)S(6)} %copy.8.reach), custom_call_target="tpu_custom_call" | custom-call | flops 805306368 | bytes 6291456 | tf_op jit(solution)/shard_map/pallas_call | solution.py:221
  45.1 0.7 %copy.9 = bf16[32,4096]{1,0:T(8,128)(2,1)} copy(bf16[32,4096]{1,0:T(8,128)(2,1)S(1)} %shard_map.64) | data formatting | bytes 524288
Async XLA Ops:
  0.7 1.9 %copy-start = (bf16[4096,1,384]{2,0,1:T(8,128)(2,1)S(1)}, bf16[4096,1,384]{2,0,1:T(8,128)(2,1)}, u32[]{:S(2)}) copy-start(bf16[4096,1,384]{2,0,1:T(8,128)(2,1)} %param.7) | copy-start | bytes 9437188
  2.5 1.2 %copy-start.1 = (bf16[1,128,4096]{2,1,0:T(8,128)(2,1)S(1)}, bf16[1,128,4096]{2,1,0:T(8,128)(2,1)}, u32[]{:S(2)}) copy-start(bf16[1,128,4096]{2,1,0:T(8,128)(2,1)} %param.8) | copy-start | bytes 3145732
  3.8 0.9 %copy-start.2 = (bf16[256,512]{1,0:T(8,128)(2,1)S(1)}, bf16[256,512]{1,0:T(8,128)(2,1)}, u32[]{:S(2)}) copy-start(bf16[256,512]{1,0:T(8,128)(2,1)} %tok.1) | copy-start | bytes 786436
  4.7 0.9 %copy-start.3 = (bf16[1,512,128]{2,1,0:T(8,128)(2,1)S(1)}, bf16[1,512,128]{2,1,0:T(8,128)(2,1)}, u32[]{:S(2)}) copy-start(bf16[1,512,128]{2,1,0:T(8,128)(2,1)} %param.9) | copy-start | bytes 393220
  5.6 0.7 %copy-start.4 = (s32[1,256]{1,0:T(1,128)S(1)}, s32[1,256]{1,0:T(1,128)}, u32[]{:S(2)}) copy-start(s32[1,256]{1,0:T(1,128)} %codes.1) | copy-start | bytes 3076
